TPU v7x, 128 devices: a whole 4x4x4 slice. The times are simulated.
128 devices in a mesh: chan: 8 (over y, x_lo), blk: 16 (over x_hi, z, core).
Axes of the slice: x: 4 (x_hi: 2, x_lo: 2; x = x_hi * 2 + x_lo), y: 4, z: 4, core: 2. Of those that a mesh axis runs over, the one named last changes fastest.
Arguments:
- voltages: bfloat16 [2, 16, 64, 536576], P(None, 'blk', 'chan'), may hold values from -5.5 to 5.5
- fir_taps: float32 [4, 4096], replicated, may hold values from -3 to 3
- station_flags: int32 [512], replicated, may hold values 0 or 1
- bin_offsets: int32 [256], replicated, may hold values from 0 to 3
Outputs:
- visibilities: bfloat16 [256, 2, 1024, 1024], P('chan', None, 'blk')
All inputs are finite; a program needn't handle non-finite values.
Results may differ from a plain program's by a relative error of at most 0.0034.
Values may be sent and summed in bfloat16 or wider, within the bound.
No kernel may reach another device: no remote copies, remote signals or barrier semaphores. Data moves between devices by JAX's collectives and lax.ppermute only.
A program may use at most 256 MiB of HBM per device.

v0:
```python
import math
import jax
import jax.numpy as jnp
from jax import lax
from jax.sharding import PartitionSpec as P

NFFT = 4096
KEEP = 256
TAPS = 4
FRAMES = 128


def phase_table(length, kept):
    row_index = lax.broadcasted_iota(jnp.int32, (length, kept), 0)
    column_index = lax.broadcasted_iota(jnp.int32, (length, kept), 1)
    phases = row_index * column_index % length
    angles = phases.astype(jnp.float32) * (2.0 * math.pi / length)
    cosine = jnp.cos(angles)
    sine_part = jnp.sin(angles)
    upper = jnp.stack([cosine, -sine_part], axis=1)
    lower = jnp.stack([sine_part, cosine], axis=1)
    return jnp.stack([upper, lower])


def correlate(mine, others):
    rotated = jnp.stack([-others[1], others[0]])
    real_part = jnp.einsum("pcif,pcjf->cij", mine, others, preferred_element_type=jnp.float32)
    imag_part = jnp.einsum("pcif,pcjf->cij", mine, rotated, preferred_element_type=jnp.float32)
    return jnp.stack([real_part, imag_part], axis=1)


def on_device(voltages, fir_taps, station_flags, bin_offsets):
    inputs_here = voltages.shape[2]
    chan_total = lax.axis_size("chan")
    planes = voltages.reshape(2, inputs_here, FRAMES + TAPS - 1, NFFT)
    filtered = jnp.zeros((2, inputs_here, FRAMES, NFFT), jnp.float32)
    for tap_index in range(TAPS):
        filtered = (
            filtered
            + planes[:, :, tap_index : tap_index + FRAMES, :].astype(jnp.float32)
            * fir_taps[tap_index]
        )
    first_input = (
        lax.axis_index("blk") * (inputs_here * chan_total) + lax.axis_index("chan") * inputs_here
    )
    weights = lax.dynamic_slice_in_dim(
        jnp.repeat(station_flags, 2).astype(jnp.float32), first_input, inputs_here, 0
    )
    spectrum = jnp.einsum(
        "pifn,pnqk->qkif",
        filtered,
        phase_table(NFFT, KEEP),
        precision=lax.Precision.HIGHEST,
        preferred_element_type=jnp.float32,
    )
    spectra = (spectrum / math.sqrt(2.0 * NFFT) * weights[:, None]).astype(jnp.bfloat16)
    scales = jnp.exp2(-bin_offsets.astype(jnp.float32)) / FRAMES
    local = lax.all_to_all(spectra, "chan", split_axis=1, concat_axis=2, tiled=True)
    group_channels = local.shape[1]
    sums = correlate(local, lax.all_gather(local, "blk", axis=2, tiled=True))
    first_channel = lax.axis_index("chan") * group_channels
    factor = lax.dynamic_slice_in_dim(scales, first_channel, group_channels, 0)
    return (sums * factor[:, None, None, None]).astype(jnp.bfloat16)


def solution(mesh):
    in_specs = (P(None, "blk", "chan", None), P(), P(), P())
    out_specs = P("chan", None, "blk", None)
    return jax.shard_map(
        on_device, mesh=mesh, in_specs=in_specs, out_specs=out_specs, check_vma=False
    )
```

profile of v0, /device:TPU:1, one launch (start us, length us, event | category | flops | bytes accessed | tf_op | source)
XLA Modules:
  0.0 397.2 jit_solution(11936473295137632323)
XLA Ops:
  6.5 0.0 copy-start.2
  6.5 0.0 copy-start.1
  6.5 0.0 all-gather.2.cloned.1.call-start
  6.5 16.5 %fusion.40 = f32[4096,1,256]{0,2,1:T(8,128)} fusion(), kind=kLoop, calls=%fused_computation.48 | loop fusion | flops 15728640 | bytes 4194304 | tf_op jit(solution)/shard_map/neg | solution.py:20
  23.1 17.6 %fusion.38 = (f32[4096,1,256]{0,2,1:T(8,128)}, f32[4096,1,256]{0,2,1:T(8,128)}) fusion(), kind=kLoop, calls=%fused_computation.46 | loop fusion | flops 14680064 | bytes 8388608 | tf_op jit(solution)/shard_map/sin | solution.py:19
  40.6 0.0 copy-done.2
  40.7 0.0 copy-done.1
  40.7 0.1 broadcast_in_dim.4
  40.9 0.2 convert_element_type.58
  41.0 44.0 %fusion.45 = (bf16[2,8,128,4096]{3,1,2,0:T(8,128)(2,1)}, bf16[2,8,128,4096]{3,1,2,0:T(8,128)(2,1)}, bf16[2,8,128,4096]{3,1,2,0:T(8,128)(2,1)}, bf16[2,8,128,4096]{3,1,2,0:T(8,128)(2,1)}) fusion(bf16[2,8,131,4096]{3,1,2,0:T(8,128)(2,1)} %bitcast.53), kind=kLoop, calls=%fused_computation.54 | loop fusion | bytes 134217728 | tf_op jit(solution)/shard_map/slice | solution.py:40
  85.0 0.1 dynamic-slice_multiply_fusion
  85.1 0.0 copy-start
  85.1 13.3 %maximum_bitcast_fusion.2 = (f32[1,4096,2,256]{1,3,0,2:T(8,128)}, f32[1,4096,2,256]{1,3,0,2:T(8,128)}) fusion(f32[4096,1,256]{0,2,1:T(8,128)} %fusion.40, f32[4096,1,256]{0,2,1:T(8,128)} %get-tuple-element.18, f32[4096,1,256]{0,2,1:T(8,128)} %get-tuple-element.17), kind=kLoop, calls=%fused_computation.31 | loop fusion | flops 4194304 | bytes 29360128 | tf_op jit(solution)/shard_map/stack | solution.py:22
  98.5 3.0 copy-done
  101.4 0.0 copy-start.3
  101.4 100.0 %fusion.37 = bf16[2,256,8,128]{3,1,2,0:T(8,128)(2,1)S(1)} fusion(bf16[2,8,128,4096]{3,1,2,0:T(8,128)(2,1)} %get-tuple-element.8, bf16[2,8,128,4096]{3,1,2,0:T(8,128)(2,1)} %get-tuple-element.6, bf16[2,8,128,4096]{3,1,2,0:T(8,128)(2,1)} %get-tuple-element.7, bf16[2,8,128,4096]{3,1,2,0:T(8,128)(2,1)S(1)} %copy-done, f32[4096]{0:T(1024)S(1)} %bitcast.60, ...), kind=kOutput, calls=%fused_computation.45 | convolution fusion | flops 51637125120 | bytes 85000224 | tf_op jit(solution)/shard_map/pifn,pnqk->qkif/dot_general | solution.py:49
  201.4 0.7 copy.24
  202.1 20.7 %all_to_all.18 = bf16[2,256,8,128]{3,2,0,1:T(8,128)(2,1)S(1)} all-to-all(bf16[2,256,8,128]{3,2,0,1:T(8,128)(2,1)S(1)} %copy.24), channel_id=1, replica_groups=mesh['chan'=8,'blk'=16] {'chan'}, dimensions={1} | all-to-all | bytes 2097152 | tf_op jit(solution)/shard_map/all_to_all | solution.py:58
  222.8 1.3 copy.74
  224.0 0.0 all-gather.2.cloned.1.call-update
  224.1 0.0 copy-done.3
  224.1 0.1 dynamic_slice.7
  224.2 111.1 %all-gather.2.cloned.1.call-done = bf16[2,32,1024,128]{3,2,0,1:T(8,128)(2,1)} async-done(((bf16[2,32,64,128]{3,2,0,1:T(8,128)(2,1)}), bf16[2,32,1024,128]{3,2,0,1:T(8,128)(2,1)}) %all-gather.2.cloned.1.call-update) | async-done | bytes 16777232 | tf_op jit(solution)/shard_map/all_gather | solution.py:60
  335.2 11.7 %slice_negate_fusion = (bf16[1,32,1024,128]{3,2,0,1:T(8,128)(2,1)}, bf16[1,32,1024,128]{3,2,0,1:T(8,128)(2,1)}) fusion(bf16[2,32,1024,128]{3,2,0,1:T(8,128)(2,1)} %all-gather.2.cloned.1.call-done), kind=kLoop, calls=%fused_computation.30 | loop fusion | flops 4194304 | bytes 33554432 | tf_op jit(solution)/shard_map/neg | solution.py:26
  346.9 10.7 %fusion.34 = f32[32,1,64,1024]{3,2,0,1:T(8,128)} fusion(bf16[1,32,1024,128]{3,2,0,1:T(8,128)(2,1)} %get-tuple-element.10, bf16[1,32,1024,128]{3,2,0,1:T(8,128)(2,1)} %get-tuple-element.9, bf16[2,8,32,8,128]{4,3,0,2,1:T(8,128)(2,1)S(1)} %bitcast.55), kind=kOutput, calls=%fused_computation.43 | convolution fusion | flops 1082130432 | bytes 26214400 | tf_op jit(solution)/shard_map/pcif,pcjf->cij/dot_general | solution.py:28
  357.6 14.3 %convolution_bitcast_fusion = f32[32,1,64,1024]{3,2,0,1:T(8,128)} fusion(bf16[2,32,1024,128]{3,2,0,1:T(8,128)(2,1)} %all-gather.2.cloned.1.call-done, bf16[2,8,32,8,128]{4,3,0,2,1:T(8,128)(2,1)S(1)} %bitcast.56), kind=kOutput, calls=%fused_computation.42 | convolution fusion | flops 1073741824 | bytes 26214400 | tf_op jit(solution)/shard_map/pcif,pcjf->cij/dot_general | solution.py:27
  371.9 9.8 %fusion.19 = bf16[32,2,64,1024]{3,2,0,1:T(8,128)(2,1)} fusion(f32[32,1,64,1024]{3,2,0,1:T(8,128)} %fusion.34, f32[32,1,64,1024]{3,2,0,1:T(8,128)} %convolution_bitcast_fusion, f32[32]{0:T(128)S(1)} %dynamic_slice.7), kind=kLoop, calls=%fused_computation.21 | loop fusion | flops 12582912 | bytes 25165952 | tf_op jit(solution)/shard_map/convert_element_type | solution.py:63
  381.8 8.6 %copy.26 = bf16[32,2,64,1024]{3,2,1,0:T(8,128)(2,1)} copy(bf16[32,2,64,1024]{3,2,0,1:T(8,128)(2,1)} %fusion.19) | data formatting | bytes 16777216 | tf_op jit(solution)/shard_map/convert_element_type | solution.py:63
  (3 shorter events, 0.1 us)
Async XLA Ops:
  6.5 34.1 %copy-start.2 = (s32[512]{0:T(512)S(1)}, s32[512]{0:T(512)}, u32[]{:S(2)}) copy-start(s32[512]{0:T(512)} %param.6) | copy-start | bytes 6148
  6.5 34.1 %copy-start.1 = (f32[4,4096]{1,0:T(4,128)S(1)}, f32[4,4096]{1,0:T(4,128)}, u32[]{:S(2)}) copy-start(f32[4,4096]{1,0:T(4,128)} %param.5) | copy-start | bytes 196612
  6.5 328.7 %all-gather.2.cloned.1.call-start = ((), (), s32[]{:S(2)}) async-start(), calls=%async_computation.1 | async-start | bytes 17825792 | tf_op jit(solution)/shard_map/all_gather | solution.py:60
  85.1 16.3 %copy-start = (bf16[2,8,128,4096]{3,1,2,0:T(8,128)(2,1)S(1)}, bf16[2,8,128,4096]{3,1,2,0:T(8,128)(2,1)}, u32[]{:S(2)}) copy-start(bf16[2,8,128,4096]{3,1,2,0:T(8,128)(2,1)} %get-tuple-element.5) | copy-start | bytes 50331652
  101.4 122.6 %copy-start.3 = (s32[256]{0:T(256)S(1)}, s32[256]{0:T(256)}, u32[]{:S(2)}) copy-start(s32[256]{0:T(256)} %param.7) | copy-start | bytes 3076
Sparse Core Ops, SparseCore 0:
  224.2 110.9 all-gather.1
where the time goes:
time: 397 us
  matrix products  125 us (31%)
  waiting for transfers between devices  111 us (28%)
  other arithmetic  69 us (17%)
  local copies, waits for them, and re-layouts  57.9 us (15%)
  blocking collectives  20.7 us (5%)
  between operations  13.5 us (3%)
    all_gather x1, waiting for transfers between devices, on_device(): sums = correlate(local, lax.all_gather(local, 'blk', axis=2, tiled=True))  111 us
    dot_general x1, matrix products, on_device(): jnp.einsum('pifn,pnqk->qkif', filtered, phase_table(NFFT, KEEP), precisio...  100 us
    slice x1, local copies, waits for them, and re-layouts, on_device(): planes[:, :, tap_index:tap_index + FRAMES, :].astype(jnp.float32)  44 us
    all_to_all x1, blocking collectives, on_device(): lax.all_to_all(spectra, 'chan', split_axis=1, concat_axis=2, tiled=True)  20.7 us
    sin x1, other arithmetic, phase_table(): sine_part = jnp.sin(angles)  17.6 us
    neg x1, other arithmetic, phase_table(): upper = jnp.stack([cosine, -sine_part], axis=1)  16.5 us
    dot_general x1, matrix products, correlate(): jnp.einsum('pcif,pcjf->cij', mine, others, preferred_element_type=jnp.flo...  14.3 us
    another operation x1, other arithmetic, phase_table(): return jnp.stack([upper, lower])  13.3 us
  transfers between devices with their start and end apart: 1, of which 1 were waited for; matrix products, arithmetic and copies ran while one was open for 0% of the time, Pallas kernels for 0%

commit v1 on v0

--- a/solution.py
+++ b/solution.py
@@ -3,6 +3,7 @@
 import jax.numpy as jnp
 from jax import lax
 from jax.sharding import PartitionSpec as P
+from jax.lax import all_to_all, axis_size
 
 NFFT = 4096
 KEEP = 256
@@ -57,7 +58,13 @@
     scales = jnp.exp2(-bin_offsets.astype(jnp.float32)) / FRAMES
     local = lax.all_to_all(spectra, "chan", split_axis=1, concat_axis=2, tiled=True)
     group_channels = local.shape[1]
-    sums = correlate(local, lax.all_gather(local, "blk", axis=2, tiled=True))
+    sums = correlate(
+        local,
+        jnp.concatenate(
+            all_to_all(jnp.stack([local for _ in range(axis_size("blk"))], axis=0), "blk", 0, 0),
+            axis=2,
+        ),
+    )
     first_channel = lax.axis_index("chan") * group_channels
     factor = lax.dynamic_slice_in_dim(scales, first_channel, group_channels, 0)
     return (sums * factor[:, None, None, None]).astype(jnp.bfloat16)

time: 397 us -> 579 us (1.46)
  waiting for transfers between devices: 111 us -> 254 us
  local copies, waits for them, and re-layouts: 57.9 us -> 96.7 us
  between operations: 13.5 us -> 0.09 us
  starting transfers between devices: 0.01 us -> 9.49 us
    all_to_all x0 -> x1, waiting for transfers between devices: none -> 254 us  [on_device(): all_to_all(jnp.stack([local for _ in range(axis_size('blk'))], axis=0), '...]
    all_gather x1 -> x0, waiting for transfers between devices: 111 us -> none  [on_device(): sums = correlate(local, lax.all_gather(local, 'blk', axis=2, tiled=True))]
    reshape x0 -> x1, local copies, waits for them, and re-layouts: none -> 14 us  [on_device(): jnp.concatenate(all_to_all(jnp.stack([local for _ in range(axis_size('blk...]
    slice x0 -> x1, local copies, waits for them, and re-layouts: none -> 9.92 us  [correlate(): rotated = jnp.stack([-others[1], others[0]])]
    neg x0 -> x1, local copies, waits for them, and re-layouts: none -> 9.6 us  [correlate(): rotated = jnp.stack([-others[1], others[0]])]
    all_to_all x0 -> x1, starting transfers between devices: none -> 9.49 us  [on_device(): all_to_all(jnp.stack([local for _ in range(axis_size('blk'))], axis=0), '...]
    another operation x0 -> x1, local copies, waits for them, and re-layouts: none -> 6.27 us  [on_device(): jnp.stack([local for _ in range(axis_size('blk'))], axis=0)]
where the time goes in v1:
time: 579 us; the launch traced here: 573 us
  waiting for transfers between devices  254 us (44%)
  matrix products  125 us (22%)
  local copies, waits for them, and re-layouts  96.7 us (17%)
  other arithmetic  67.3 us (12%)
  blocking collectives  20.7 us (4%)
  starting transfers between devices  9.49 us (2%)
    all_to_all x1, waiting for transfers between devices, on_device(): all_to_all(jnp.stack([local for _ in range(axis_size('blk'))], axis=0), '...  254 us
    dot_general x1, matrix products, on_device(): jnp.einsum('pifn,pnqk->qkif', filtered, phase_table(NFFT, KEEP), precisio...  100 us
    slice x1, local copies, waits for them, and re-layouts, on_device(): planes[:, :, tap_index:tap_index + FRAMES, :].astype(jnp.float32)  44 us
    all_to_all x1, blocking collectives, on_device(): lax.all_to_all(spectra, 'chan', split_axis=1, concat_axis=2, tiled=True)  20.7 us
    sin x1, other arithmetic, phase_table(): sine_part = jnp.sin(angles)  17.5 us
    neg x1, other arithmetic, phase_table(): upper = jnp.stack([cosine, -sine_part], axis=1)  16.5 us
    dot_general x1, matrix products, correlate(): jnp.einsum('pcif,pcjf->cij', mine, others, preferred_element_type=jnp.flo...  14.1 us
    reshape x1, local copies, waits for them, and re-layouts, on_device(): jnp.concatenate(all_to_all(jnp.stack([local for _ in range(axis_size('blk...  14 us
  transfers between devices with their start and end apart: 1, of which 1 were waited for; matrix products, arithmetic and copies ran while one was open for 0% of the time, Pallas kernels for 0%

profile of v1, /device:TPU:1, one launch (start us, length us, event | category | flops | bytes accessed | tf_op | source)
XLA Modules:
  0.0 573.4 jit_solution(1268391405482961371)
XLA Ops:
  0.0 0.0 copy-start.2
  0.0 0.0 copy-start.1
  0.0 16.5 %fusion.40 = f32[4096,1,256]{0,2,1:T(8,128)} fusion(), kind=kLoop, calls=%fused_computation.48 | loop fusion | flops 15728640 | bytes 4194304 | tf_op jit(solution)/shard_map/neg | solution.py:21
  16.5 17.5 %fusion.38 = (f32[4096,1,256]{0,2,1:T(8,128)}, f32[4096,1,256]{0,2,1:T(8,128)}) fusion(), kind=kLoop, calls=%fused_computation.46 | loop fusion | flops 14680064 | bytes 8388608 | tf_op jit(solution)/shard_map/sin | solution.py:20
  34.1 0.0 copy-done.2
  34.1 0.0 copy-done.1
  34.1 0.1 broadcast_in_dim.4
  34.3 0.2 convert_element_type.58
  34.4 44.0 %fusion.45 = (bf16[2,8,128,4096]{3,1,2,0:T(8,128)(2,1)}, bf16[2,8,128,4096]{3,1,2,0:T(8,128)(2,1)}, bf16[2,8,128,4096]{3,1,2,0:T(8,128)(2,1)}, bf16[2,8,128,4096]{3,1,2,0:T(8,128)(2,1)}) fusion(bf16[2,8,131,4096]{3,1,2,0:T(8,128)(2,1)} %bitcast.57), kind=kLoop, calls=%fused_computation.54 | loop fusion | bytes 134217728 | tf_op jit(solution)/shard_map/slice | solution.py:41
  78.5 0.1 dynamic-slice_multiply_fusion
  78.5 0.0 copy-start
  78.6 13.5 %maximum_bitcast_fusion.2 = (f32[1,4096,2,256]{1,3,0,2:T(8,128)}, f32[1,4096,2,256]{1,3,0,2:T(8,128)}) fusion(f32[4096,1,256]{0,2,1:T(8,128)} %fusion.40, f32[4096,1,256]{0,2,1:T(8,128)} %get-tuple-element.18, f32[4096,1,256]{0,2,1:T(8,128)} %get-tuple-element.17), kind=kLoop, calls=%fused_computation.31 | loop fusion | flops 4194304 | bytes 29360128 | tf_op jit(solution)/shard_map/stack | solution.py:23
  92.0 2.9 copy-done
  94.9 100.0 %fusion.37 = bf16[2,256,8,128]{3,1,2,0:T(8,128)(2,1)S(1)} fusion(bf16[2,8,128,4096]{3,1,2,0:T(8,128)(2,1)} %get-tuple-element.8, bf16[2,8,128,4096]{3,1,2,0:T(8,128)(2,1)} %get-tuple-element.6, bf16[2,8,128,4096]{3,1,2,0:T(8,128)(2,1)} %get-tuple-element.7, bf16[2,8,128,4096]{3,1,2,0:T(8,128)(2,1)S(1)} %copy-done, f32[4096]{0:T(1024)S(1)} %bitcast.69, ...), kind=kOutput, calls=%fused_computation.45 | convolution fusion | flops 51637125120 | bytes 85000224 | tf_op jit(solution)/shard_map/pifn,pnqk->qkif/dot_general | solution.py:50
  194.8 0.7 copy.24
  195.5 20.7 %all_to_all.23 = bf16[2,256,8,128]{3,2,0,1:T(8,128)(2,1)S(1)} all-to-all(bf16[2,256,8,128]{3,2,0,1:T(8,128)(2,1)S(1)} %copy.24), channel_id=1, replica_groups=mesh['chan'=8,'blk'=16] {'chan'}, dimensions={1} | all-to-all | bytes 2097152 | tf_op jit(solution)/shard_map/all_to_all | solution.py:59
  216.2 0.3 copy.77
  216.5 6.3 %stack.25 = bf16[16,2,32,64,128]{4,3,1,2,0:T(8,128)(2,1)} broadcast(bf16[2,32,64,128]{3,2,0,1:T(8,128)(2,1)S(1)} %bitcast.66), dimensions={1,2,3,4} | broadcast | bytes 17825792 | tf_op jit(solution)/shard_map/stack | solution.py:64
  222.8 0.0 copy-start.3
  222.8 9.5 %all-to-all-start.1 = ((bf16[16,2,32,64,128]{4,3,1,2,0:T(8,128)(2,1)}), bf16[16,2,32,64,128]{4,3,1,2,0:T(8,128)(2,1)}, u32[]{:S(2)}, u32[]{:S(2)}) async-start(bf16[16,2,32,64,128]{4,3,1,2,0:T(8,128)(2,1)} %stack.25), calls=%async_computation.1 | async-start | bytes 33554432 | tf_op jit(solution)/shard_map/all_to_all | solution.py:64
  232.3 0.0 copy-done.3
  232.3 0.1 dynamic_slice.7
  232.4 254.3 %all-to-all-done.1 = bf16[16,2,32,64,128]{4,3,1,2,0:T(8,128)(2,1)} async-done(((bf16[16,2,32,64,128]{4,3,1,2,0:T(8,128)(2,1)}), bf16[16,2,32,64,128]{4,3,1,2,0:T(8,128)(2,1)}, u32[]{:S(2)}, u32[]{:S(2)}) %all-to-all-start.1) | async-done | bytes 16777248 | tf_op jit(solution)/shard_map/all_to_all | solution.py:64
  486.6 14.0 %copy.26 = bf16[2,32,16,64,128]{4,3,2,0,1:T(8,128)(2,1)} copy(bf16[2,32,16,64,128]{4,3,0,1,2:T(8,128)(2,1)} %bitcast.17) | data formatting | bytes 33554432 | tf_op jit(solution)/shard_map/reshape | solution.py:63
  500.7 11.7 %slice_negate_fusion = (bf16[1,32,16,64,128]{4,3,0,1,2:T(8,128)(2,1)}, bf16[1,32,16,64,128]{4,3,0,1,2:T(8,128)(2,1)}) fusion(bf16[2,32,16,64,128]{4,3,0,1,2:T(8,128)(2,1)} %bitcast.17), kind=kLoop, calls=%fused_computation.30 | loop fusion | flops 4194304 | bytes 33554432 | tf_op jit(solution)/shard_map/neg | solution.py:27
  512.4 14.1 %convolution_bitcast_fusion = f32[32,1,64,1024]{3,2,0,1:T(8,128)} fusion(bf16[2,32,1024,128]{3,2,0,1:T(8,128)(2,1)} %bitcast.58, bf16[2,8,32,8,128]{4,3,0,2,1:T(8,128)(2,1)S(1)} %bitcast.62), kind=kOutput, calls=%fused_computation.42 | convolution fusion | flops 1073741824 | bytes 26214400 | tf_op jit(solution)/shard_map/pcif,pcjf->cij/dot_general | solution.py:28
  526.5 9.6 %copy.27 = bf16[1,32,16,64,128]{4,3,2,1,0:T(8,128)(2,1)} copy(bf16[1,32,16,64,128]{4,3,0,1,2:T(8,128)(2,1)} %get-tuple-element.9) | data formatting | bytes 16777216 | tf_op jit(solution)/shard_map/neg | solution.py:27
  536.1 0.0 slice-start
  536.2 9.9 %copy.28 = bf16[1,32,16,64,128]{4,3,2,1,0:T(8,128)(2,1)} copy(bf16[1,32,16,64,128]{4,3,0,1,2:T(8,128)(2,1)} %get-tuple-element.10) | data formatting | bytes 16777216 | tf_op jit(solution)/shard_map/slice | solution.py:27
  546.1 0.0 slice-start.1
  546.1 10.8 %fusion.34 = f32[32,1,64,1024]{3,2,0,1:T(8,128)} fusion(bf16[1,32,1024,128]{3,2,0,1:T(8,128)(2,1)} %bitcast.65, bf16[1,32,1024,128]{3,2,0,1:T(8,128)(2,1)} %bitcast.64, bf16[2,8,32,8,128]{4,3,0,2,1:T(8,128)(2,1)S(1)} %bitcast.63), kind=kOutput, calls=%fused_computation.43 | convolution fusion | flops 1082130432 | bytes 26214400 | tf_op jit(solution)/shard_map/pcif,pcjf->cij/dot_general | solution.py:29
  556.9 0.0 slice-done
  556.9 0.0 slice-done.1
  556.9 7.9 %fusion.19 = bf16[32,2,64,1024]{3,2,0,1:T(8,128)(2,1)} fusion(f32[32,1,64,1024]{3,2,0,1:T(8,128)} %fusion.34, f32[32,1,64,1024]{3,2,0,1:T(8,128)S(1)} %bitcast.60, f32[32]{0:T(128)S(1)} %dynamic_slice.7), kind=kLoop, calls=%fused_computation.21 | loop fusion | flops 12582912 | bytes 25165952 | tf_op jit(solution)/shard_map/convert_element_type | solution.py:70
  564.9 8.6 %copy.29 = bf16[32,2,64,1024]{3,2,1,0:T(8,128)(2,1)} copy(bf16[32,2,64,1024]{3,2,0,1:T(8,128)(2,1)} %fusion.19) | data formatting | bytes 16777216 | tf_op jit(solution)/shard_map/convert_element_type | solution.py:70
  (4 shorter events, 0.1 us)
Async XLA Ops:
  0.0 34.1 %copy-start.2 = (s32[512]{0:T(512)S(1)}, s32[512]{0:T(512)}, u32[]{:S(2)}) copy-start(s32[512]{0:T(512)} %param.6) | copy-start | bytes 6148
  0.0 34.1 %copy-start.1 = (f32[4,4096]{1,0:T(4,128)S(1)}, f32[4,4096]{1,0:T(4,128)}, u32[]{:S(2)}) copy-start(f32[4,4096]{1,0:T(4,128)} %param.5) | copy-start | bytes 196612
  78.5 16.3 %copy-start = (bf16[2,8,128,4096]{3,1,2,0:T(8,128)(2,1)S(1)}, bf16[2,8,128,4096]{3,1,2,0:T(8,128)(2,1)}, u32[]{:S(2)}) copy-start(bf16[2,8,128,4096]{3,1,2,0:T(8,128)(2,1)} %get-tuple-element.5) | copy-start | bytes 50331652
  222.8 9.5 %copy-start.3 = (s32[256]{0:T(256)S(1)}, s32[256]{0:T(256)}, u32[]{:S(2)}) copy-start(s32[256]{0:T(256)} %param.7) | copy-start | bytes 3076
  222.8 263.9 %all-to-all-start.1 = ((bf16[16,2,32,64,128]{4,3,1,2,0:T(8,128)(2,1)}), bf16[16,2,32,64,128]{4,3,1,2,0:T(8,128)(2,1)}, u32[]{:S(2)}, u32[]{:S(2)}) async-start(bf16[16,2,32,64,128]{4,3,1,2,0:T(8,128)(2,1)} %stack.25), calls=%async_computation.1 | async-start | bytes 33554432 | tf_op jit(solution)/shard_map/all_to_all | solution.py:64
  536.1 20.8 %slice-start = ((s8[8388608]{0:T(1024)(128)(4,1)}), s8[4194304]{0:T(1024)(128)(4,1)S(1)}, s32[]{:S(2)}) async-start(s8[8388608]{0:T(1024)(128)(4,1)} %bitcast.59), calls=%async_computation.2 | async-start | bytes 8388608
  546.1 10.8 %slice-start.1 = ((s8[8388608]{0:T(1024)(128)(4,1)}), s8[4194304]{0:T(1024)(128)(4,1)S(1)}, s32[]{:S(2)}) async-start(s8[8388608]{0:T(1024)(128)(4,1)} %bitcast.59), calls=%async_computation.3 | async-start | bytes 8388608
